TPU v7x, 512 devices: a whole 4x8x8 slice. The times are simulated.
512 devices in a mesh: pa: 32 (over x, y), pb: 16 (over z, core).
Axes of the slice: x: 4, y: 8, z: 8, core: 2. Of those that a mesh axis runs over, the one named last changes fastest.
Arguments:
- queries: bfloat16 [65536, 1024], P(('pa', 'pb')), may hold values from -900 to 900
- batch_hidden: bfloat16 [8192, 1024], P(('pa', 'pb')), may hold values from -6 to 6
- pool_hidden: bfloat16 [262144, 1024], P(('pa', 'pb')), may hold values from -6 to 6
- projection: bfloat16 [1024, 1024], replicated, may hold values from -0.1875 to 0.1875
- hard_ids: int32 [65536, 16], P(('pa', 'pb')), may hold values from 0 to 8191, as said below
- query_group: int32 [65536], P(('pa', 'pb')), may hold values from 0 to 63
- labels: int32 [65536], P(('pa', 'pb')), may hold values from 0 to 63
- group_lists: int32 [64, 64], replicated, may hold values from 0 to 511, as said below
Outputs:
- query_grad: bfloat16 [65536, 1024], P(('pa', 'pb'))
- batch_hidden_grad: bfloat16 [8192, 1024], P(('pa', 'pb'))
- pool_hidden_grad: bfloat16 [262144, 1024], P(('pa', 'pb'))
Inputs may be any that keep to these rules, and one draw needn't show every extreme that they name: `hard_ids`: entry k of a query's list lies in [(k % 16) * 512, (k % 16 + 1) * 512); entries may repeat. `group_lists`: each row holds 64 different values.
All inputs are finite; a program needn't handle non-finite values.
Results may differ from a plain program's by a relative error of at most 0.017.
The roundings to bfloat16 on the way count: a program that leaves them out, or rounds other values in their place, can miss the bound.
Values may be sent and summed in bfloat16 or wider, within the bound.
A program may use at most 128 MiB of HBM per device.

v0:
```python
import math

import jax
import jax.numpy as jnp
from jax import lax
from jax.sharding import PartitionSpec as P

D = 1024


def pick_rows(table, wanted):
    flat = wanted.reshape(-1)
    table_iota = lax.broadcasted_iota(jnp.int32, (flat.shape[0], table.shape[0]), 1)
    selector = (flat[:, None] == table_iota).astype(jnp.bfloat16)
    found = jnp.dot(selector, table, preferred_element_type=jnp.float32).astype(table.dtype)
    return found.reshape(wanted.shape + (table.shape[1],))


def add_rows(wanted, values, count):
    flat = wanted.reshape(-1)
    row_iota = lax.broadcasted_iota(jnp.int32, (count, flat.shape[0]), 0)
    selector = (row_iota == flat[None, :]).astype(jnp.bfloat16)
    return jnp.dot(selector, values.reshape(flat.shape[0], -1), preferred_element_type=jnp.float32)


def shards(
    queries, batch_hidden, pool_hidden, projection, hard_ids, query_group, labels, group_lists
):
    score_scale = 1.0 / math.sqrt(D)
    owners = lax.axis_size("pb")
    query_rows = queries.shape[0]
    pool_count = pool_hidden.shape[0]
    hard_count = hard_ids.shape[1]
    per_owner = hard_count // owners
    group_size = group_lists.shape[1]
    group_total = group_lists.shape[0]
    dims = (((1,), (1,)), ((), ()))
    batch_proj = jnp.dot(batch_hidden, projection, preferred_element_type=jnp.float32).astype(
        jnp.bfloat16
    )
    pool_proj = jnp.dot(pool_hidden, projection, preferred_element_type=jnp.float32).astype(
        jnp.bfloat16
    )
    column = lax.all_gather(batch_proj, "pa", axis=0, tiled=True)
    column_count = column.shape[0]
    dense = lax.dot_general(queries, column, dims, preferred_element_type=jnp.float32) * score_scale
    group_iota = lax.broadcasted_iota(jnp.int32, (query_rows, group_total, group_size), 1)
    chosen = jnp.sum(
        jnp.where(query_group[:, None, None] == group_iota, group_lists[None, :, :], 0), axis=1
    )
    column_iota = lax.broadcasted_iota(jnp.int32, (query_rows, group_size, column_count), 2)
    member = chosen[:, :, None] == column_iota
    group_scores = jnp.sum(jnp.where(member, dense[:, None, :], 0.0), axis=2)
    owner_of = lax.broadcasted_iota(jnp.int32, hard_ids.shape, 1) % owners
    local_rows = hard_ids - owner_of * pool_count
    requests = (
        local_rows.reshape(query_rows, per_owner, owners)
        .transpose(2, 0, 1)
        .reshape(owners, query_rows * per_owner)
    )
    received = lax.all_to_all(requests, "pb", split_axis=0, concat_axis=0, tiled=True)
    copies = lax.all_gather(queries, "pb", axis=0, tiled=True).reshape(owners, query_rows, D)
    picked = pick_rows(pool_proj, received).reshape(owners, query_rows, per_owner, D)
    owner_scores = (
        jnp.einsum("sid,sijd->sij", copies, picked, preferred_element_type=jnp.float32)
        * score_scale
    )
    returned = lax.all_to_all(owner_scores, "pb", split_axis=0, concat_axis=0, tiled=True)
    hard_scores = returned.transpose(1, 2, 0).reshape(query_rows, hard_count)
    scores = jnp.concatenate([group_scores, hard_scores], axis=1)
    likely = jax.nn.softmax(scores, axis=1)
    positions = lax.broadcasted_iota(jnp.int32, scores.shape, 1)
    target = (positions == labels[:, None]).astype(jnp.float32)
    dscore = (likely - target).astype(jnp.bfloat16)
    grad_group = dscore[:, :group_size]
    grad_hard = dscore[:, group_size:].reshape(query_rows, per_owner, owners).transpose(2, 0, 1)
    dense_grad = jnp.einsum(
        "ic,icr->ir", grad_group, member.astype(jnp.bfloat16), preferred_element_type=jnp.float32
    ).astype(jnp.bfloat16)
    group_term = jnp.dot(dense_grad, column, preferred_element_type=jnp.float32)
    batch_part = (
        lax.dot_general(
            dense_grad, queries, (((0,), (0,)), ((), ())), preferred_element_type=jnp.float32
        )
        * score_scale
    )
    batch_grad = lax.psum_scatter(batch_part, "pa", scatter_dimension=0, tiled=True)
    sent_back = lax.all_to_all(grad_hard, "pb", split_axis=0, concat_axis=0, tiled=True)
    contrib = (
        score_scale
        * sent_back.astype(jnp.float32)[..., None]
        * copies.astype(jnp.float32)[:, :, None, :]
    )
    contrib = contrib.astype(jnp.bfloat16)
    pool_grad = add_rows(received, contrib, pool_count)
    owner_term = jnp.einsum("sij,sijd->sid", sent_back, picked, preferred_element_type=jnp.float32)
    gathered_terms = lax.all_to_all(owner_term, "pb", split_axis=0, concat_axis=0, tiled=True)
    hard_term = jnp.sum(gathered_terms, axis=0)
    query_grad = (score_scale * (group_term + hard_term)).astype(jnp.bfloat16)
    batch_hidden_grad = lax.dot_general(
        batch_grad.astype(jnp.bfloat16), projection, dims, preferred_element_type=jnp.float32
    ).astype(jnp.bfloat16)
    pool_hidden_grad = lax.dot_general(
        pool_grad.astype(jnp.bfloat16), projection, dims, preferred_element_type=jnp.float32
    ).astype(jnp.bfloat16)
    return (query_grad, batch_hidden_grad, pool_hidden_grad)


def solution(mesh):
    return jax.shard_map(
        shards,
        mesh=mesh,
        in_specs=(
            P(("pa", "pb"), None),
            P(("pa", "pb"), None),
            P(("pa", "pb"), None),
            P(),
            P(("pa", "pb"), None),
            P(("pa", "pb")),
            P(("pa", "pb")),
            P(),
        ),
        out_specs=(P(("pa", "pb"), None), P(("pa", "pb"), None), P(("pa", "pb"), None)),
        check_vma=False,
    )
```

profile of v0, /device:TPU:6, one launch (start us, length us, event | category | flops | bytes accessed | tf_op | source)
XLA Modules:
  0.0 425.0 jit_solution(14734959064814197751)
XLA Ops:
  7.2 0.0 copy-start
  7.2 0.0 all-gather.3.cloned.1.call-start
  7.2 1.5 copy-done
  8.8 1.8 convolution_convert_fusion.3
  10.5 0.0 all-gather.3.cloned.1.call-update
  10.5 0.0 all-gather.5.cloned.1.call-start
  10.6 0.7 all-gather.5.cloned.1.call-update
  11.3 1.4 multiply_subtract_fusion
  12.7 10.4 %all-to-all-start = ((s32[16,1,128]{2,1,0:T(1,128)}), s32[16,1,128]{2,1,0:T(1,128)S(1)}, u32[]{:S(2)}, u32[]{:S(2)}) async-start(s32[16,1,128]{2,1,0:T(1,128)} %bitcast.3), calls=%async_computation | async-start | bytes 16384 | tf_op jit(solution)/shard_map/all_to_all | solution.py:61
  23.1 1.4 select_reduce_fusion.1
  24.6 0.1 copy.16
  24.7 6.0 %all-to-all-done = s32[16,1,128]{2,1,0:T(1,128)S(1)} async-done(((s32[16,1,128]{2,1,0:T(1,128)}), s32[16,1,128]{2,1,0:T(1,128)S(1)}, u32[]{:S(2)}, u32[]{:S(2)}) %all-to-all-start) | async-done | bytes 8224 | tf_op jit(solution)/shard_map/all_to_all | solution.py:61
  30.6 0.0 copy-start.2
  30.6 6.6 %fusion.6 = bf16[2048,1024]{1,0:T(8,128)(2,1)} fusion(s32[2048]{0:T(1024)S(1)} %bitcast.42, bf16[512,1024]{1,0:T(8,128)(2,1)} %param.10, bf16[1024,1024]{1,0:T(8,128)(2,1)S(1)} %copy-done), kind=kOutput, calls=%fused_computation.13 | convolution fusion | flops 3224895488 | bytes 7348224 | tf_op jit(solution)/shard_map/dot_general | solution.py:15
  37.2 59.4 %all-gather.3.cloned.1.call-done = bf16[512,1024]{1,0:T(8,128)(2,1)} async-done(((bf16[16,1024]{1,0:T(8,128)(2,1)}), bf16[512,1024]{1,0:T(8,128)(2,1)}) %all-gather.3.cloned.1.call-update) | async-done | bytes 1048592 | tf_op jit(solution)/shard_map/all_gather | solution.py:44
  96.7 0.0 copy-done.2
  96.7 1.7 fusion.12
  98.3 0.1 copy.17
  98.5 45.1 %all-gather.5.cloned.1.call-done = bf16[2048,1024]{1,0:T(8,128)(2,1)} async-done(((bf16[128,1024]{1,0:T(8,128)(2,1)}), bf16[2048,1024]{1,0:T(8,128)(2,1)}) %all-gather.5.cloned.1.call-update) | async-done | bytes 4194320 | tf_op jit(solution)/shard_map/all_gather | solution.py:62
  143.6 0.0 copy-start.3
  143.6 4.6 %fusion.1 = f32[16,128]{1,0:T(8,128)S(1)} fusion(bf16[16,128,1024]{2,1,0:T(8,128)(2,1)} %bitcast.36, bf16[16,128,1024]{2,1,0:T(8,128)(2,1)} %bitcast.37), kind=kLoop, calls=%fused_computation.5 | loop fusion | flops 8386560 | bytes 8396800 | tf_op jit(solution)/shard_map/sid,sijd->sij/dot_general | solution.py:65
  148.2 0.6 broadcast_multiply_fusion.1
  148.8 4.2 all-to-all-start.1
  153.1 3.2 select_reduce_fusion
  156.3 0.1 reduce_max.20
  156.4 4.2 all-to-all-done.1
  160.6 0.1 copy.18
  160.7 0.2 fusion.16
  160.9 0.0 copy-done.3
  160.9 0.1 subtract_convert_fusion
  161.1 0.1 slice.9
  161.2 0.1 copy.19
  161.3 10.4 %all_to_all.24 = bf16[16,128,1]{1,2,0:T(2,128)(2,1)S(1)} all-to-all(bf16[16,128,1]{1,2,0:T(2,128)(2,1)S(1)} %copy.20), channel_id=1, replica_groups=mesh['pa'=32,'pb'=16] {'pb'}, dimensions={0} | all-to-all | bytes 8192 | tf_op jit(solution)/shard_map/all_to_all | solution.py:88
  171.7 6.0 %convert_multiply_fusion = f32[16,128,1024]{2,1,0:T(8,128)} fusion(f32[16,128]{1,0:T(8,128)S(1)} %bitcast.40, bf16[2048,1024]{1,0:T(8,128)(2,1)} %fusion.6), kind=kLoop, calls=%fused_computation.3 | loop fusion | flops 4194304 | bytes 12591104 | tf_op jit(solution)/shard_map/sij,sijd->sid/dot_general | solution.py:96
  177.7 4.7 %all-to-all-start.3 = ((f32[16,128,1024]{2,1,0:T(8,128)}), f32[16,128,1024]{2,1,0:T(8,128)}, u32[]{:S(2)}, u32[]{:S(2)}) async-start(f32[16,128,1024]{2,1,0:T(8,128)} %convert_multiply_fusion), calls=%async_computation.3 | async-start | bytes 16777216 | tf_op jit(solution)/shard_map/all_to_all | solution.py:97
  182.4 0.2 reduce-scatter.2.cloned.1.call-start
  182.7 3.3 fusion
  186.0 1.8 convolution_multiply_fusion
  187.8 0.0 reduce-scatter.2.cloned.1.call-update
  187.8 6.7 %convolution_convert_fusion = bf16[512,1024]{1,0:T(8,128)(2,1)} fusion(bf16[1024,1024]{1,0:T(8,128)(2,1)S(1)} %copy-done, bf16[2048,1024]{1,0:T(8,128)(2,1)} %all-gather.5.cloned.1.call-done, f32[2048]{0:T(1024)S(1)} %bitcast.44, s32[2048]{0:T(1024)S(1)} %bitcast.43), kind=kOutput, calls=%fused_computation.20 | convolution fusion | flops 3229614080 | bytes 7356416 | tf_op jit(solution)/shard_map/dot_general | solution.py:103
  194.5 214.6 %reduce-scatter.2.cloned.1.call-done = f32[16,1024]{1,0:T(8,128)} async-done(((f32[512,1024]{1,0:T(8,128)}), f32[16,1024]{1,0:T(8,128)}) %reduce-scatter.2.cloned.1.call-update) | async-done | bytes 65552 | tf_op jit(solution)/shard_map/reduce_scatter | solution.py:87
  409.1 2.1 convolution_convert_fusion.2
  411.2 0.0 copy-start.1
  411.2 0.0 all-to-all-done.3
  411.2 5.2 %reduce_sum.39 = f32[128,1024]{1,0:T(8,128)} reduce(f32[16,128,1024]{2,1,0:T(8,128)} %all-to-all-done.3, f32[]{:T(128)} %constant.11.clone.1), dimensions={0}, to_apply=%region_5.6 | reduce | flops 1966080 | bytes 8912900 | tf_op jit(solution)/shard_map/reduce_sum | solution.py:98
  416.4 0.0 copy-done.1
  416.4 2.1 fusion.11
  (8 shorter events, 0.1 us)
Async XLA Ops:
  7.2 1.6 copy-start
  7.2 89.5 %all-gather.3.cloned.1.call-start = ((), (), s32[]{:S(2)}) async-start(), calls=%async_computation.5 | async-start | bytes 1081344 | tf_op jit(solution)/shard_map/all_gather | solution.py:44
  10.5 133.1 %all-gather.5.cloned.1.call-start = ((), (), s32[]{:S(2)}) async-start(), calls=%async_computation.6 | async-start | bytes 4456448 | tf_op jit(solution)/shard_map/all_gather | solution.py:62
  12.7 17.9 %all-to-all-start = ((s32[16,1,128]{2,1,0:T(1,128)}), s32[16,1,128]{2,1,0:T(1,128)S(1)}, u32[]{:S(2)}, u32[]{:S(2)}) async-start(s32[16,1,128]{2,1,0:T(1,128)} %bitcast.3), calls=%async_computation | async-start | bytes 16384 | tf_op jit(solution)/shard_map/all_to_all | solution.py:61
  30.6 66.0 %copy-start.2 = (bf16[128,1024]{1,0:T(8,128)(2,1)S(1)}, bf16[128,1024]{1,0:T(8,128)(2,1)}, u32[]{:S(2)}) copy-start(bf16[128,1024]{1,0:T(8,128)(2,1)} %param.8) | copy-start | bytes 786436
  143.6 17.3 %copy-start.3 = (s32[128]{0:T(128)S(1)}, s32[128]{0:T(128)}, u32[]{:S(2)}) copy-start(s32[128]{0:T(128)} %param.14) | copy-start | bytes 1540
  148.8 11.7 %all-to-all-start.1 = ((f32[16,128,1]{1,2,0:T(1,128)}), f32[16,128,1]{1,2,0:T(1,128)S(1)}, u32[]{:S(2)}, u32[]{:S(2)}) async-start(f32[16,128,1]{1,2,0:T(1,128)} %bitcast.7), calls=%async_computation.1 | async-start | bytes 16384 | tf_op jit(solution)/shard_map/all_to_all | solution.py:68
  177.7 233.5 %all-to-all-start.3 = ((f32[16,128,1024]{2,1,0:T(8,128)}), f32[16,128,1024]{2,1,0:T(8,128)}, u32[]{:S(2)}, u32[]{:S(2)}) async-start(f32[16,128,1024]{2,1,0:T(8,128)} %convert_multiply_fusion), calls=%async_computation.3 | async-start | bytes 16777216 | tf_op jit(solution)/shard_map/all_to_all | solution.py:97
  182.4 226.6 %reduce-scatter.2.cloned.1.call-start = ((), (), s32[]{:S(2)}) async-start(), calls=%async_computation.7 | async-start | bytes 2162688 | tf_op jit(solution)/shard_map/reduce_scatter | solution.py:87
  411.2 5.2 %copy-start.1 = (bf16[512,1024]{1,0:T(8,128)(2,1)S(1)}, bf16[512,1024]{1,0:T(8,128)(2,1)}, u32[]{:S(2)}) copy-start(bf16[512,1024]{1,0:T(8,128)(2,1)} %all-gather.3.cloned.1.call-done) | copy-start | bytes 3145732
Sparse Core Ops, SparseCore 0:
  11.8 84.8 all-gather.2
  98.8 44.7 all-gather.4
  187.9 221.1 reduce-scatter.1
where the time goes:
time: 426 us; the launch traced here: 425 us
  waiting for transfers between devices  330 us (77%)
  matrix products  26 us (6%)
  other arithmetic  22.9 us (5%)
  starting transfers between devices  19.7 us (5%)
  between operations  13.9 us (3%)
  blocking collectives  10.4 us (2%)
    reduce_scatter x1, waiting for transfers between devices, shards(): lax.psum_scatter(batch_part, 'pa', scatter_dimension=0, tiled=True)  215 us
    all_gather x1, waiting for transfers between devices, shards(): column = lax.all_gather(batch_proj, 'pa', axis=0, tiled=True)  59.4 us
    all_gather x1, waiting for transfers between devices, shards(): lax.all_gather(queries, 'pb', axis=0, tiled=True)  45.1 us
    all_to_all x1, starting transfers between devices, shards(): lax.all_to_all(requests, 'pb', split_axis=0, concat_axis=0, tiled=True)  10.4 us
    all_to_all x1, blocking collectives, shards(): lax.all_to_all(grad_hard, 'pb', split_axis=0, concat_axis=0, tiled=True)  10.4 us
  transfers between devices with their start and end apart: 6, of which 5 were waited for; matrix products, arithmetic and copies ran while one was open for 7% of the time, Pallas kernels for 0%

commit v1 on v0

v1 whole, which is shorter than its diff:
```python
import math

import jax
import jax.numpy as jnp
from jax import lax
from jax.experimental import pallas as pl
from jax.experimental.pallas import tpu as pltpu
from jax.sharding import PartitionSpec as P

MESH = pl.DeviceIdType.MESH
NX, NY, NZ = 4, 8, 8
D = 1024
QD = 128
PD = 512
IB = 16
NG = 64
GS = 64
HN = 16
NB = NX * NY * IB
SLAB = NY * IB
SUB = QD // 2
SCALE = 1.0 / math.sqrt(D)
F32 = jnp.float32
BF16 = jnp.bfloat16
LOW = -3.0e38

MIRROR = (0, 2, 1, 4, 3, 6, 5, 7)


def slot_of(direction, hops):
    if hops == 0:
        return 0
    if hops == 4:
        return 7
    return 2 * hops - 1 if direction == 0 else 2 * hops


def slot_shift(slot):
    if slot == 7:
        return 4
    hops = (slot + 1) // 2
    return (-hops if slot % 2 else hops) % NZ


def dot(a, b):
    return jnp.dot(a, b, preferred_element_type=F32)


def dot_nt(a, b):
    return lax.dot_general(a, b, (((1,), (1,)), ((), ())), preferred_element_type=F32)


def eye(n):
    same = lax.broadcasted_iota(jnp.int32, (n, n), 0) == lax.broadcasted_iota(jnp.int32, (n, n), 1)
    return jnp.where(same, 1.0, 0.0).astype(BF16)


def turn_ids(ids):
    high = (ids // 128).astype(F32).astype(BF16)
    low = (ids % 128).astype(F32).astype(BF16)
    one = eye(ids.shape[1])
    return (dot_nt(one, high) * 128.0 + dot_nt(one, low)).astype(jnp.int32)


def kernel(
    q_hbm, bh_hbm, ph_hbm, proj_hbm, ids_ref, group_ref, label_ref, lists_ref,
    qg_out, bg_out, pg_out,
    qbuf, proj, bh, ph, pool, column, ot, mask, dense, chosen,
    ids_byz, ids_in, hs_out, hs_in, d_out, d_in, rows16, idcol, dcol,
    t_buf, o_buf, rs_out, rs_in, dg, part, xr_out, xr_in, xsum, y_out, y_in, gterm,
    contrib, g_send, g_recv, g_own, gb, qg_stage, bg_stage, pg_stage,
    ld_sem, st_sem, ag_s, ag_r, rs_s, rs_r, xa_s, xa_r, xr_s, xr_r, one_s, one_r,
):
    pa = lax.axis_index("pa")
    pb = lax.axis_index("pb")
    x, y = pa // NY, pa % NY
    z, core = pb // 2, pb % 2

    def at_z(shift):
        return (pa, ((z + shift + NZ) % NZ) * 2 + core)

    def at_y(shift):
        return (x * NY + (y + shift) % NY, pb)

    def at_x(shift):
        return (((x + shift + NX) % NX) * NY + y, pb)

    partner = (pa, z * 2 + 1 - core)

    def remote(src, dst, send, recv, device):
        return pltpu.make_async_remote_copy(
            src_ref=src, dst_ref=dst, send_sem=send, recv_sem=recv, device_id=device, device_id_type=MESH
        )

    barrier = pltpu.get_barrier_semaphore()
    peers = [at_z(s) for s in range(1, NZ)] + [at_y(s) for s in range(1, NY)] + [at_x(1), at_x(-1), partner]
    for peer in peers:
        pl.semaphore_signal(barrier, inc=1, device_id=peer, device_id_type=MESH)

    loads = [
        pltpu.make_async_copy(q_hbm, qbuf.at[0], ld_sem.at[0]),
        pltpu.make_async_copy(bh_hbm, bh, ld_sem.at[1]),
        pltpu.make_async_copy(proj_hbm, proj, ld_sem.at[2]),
        pltpu.make_async_copy(ph_hbm, ph, ld_sem.at[3]),
    ]
    for load in loads:
        load.start()

    turned = turn_ids(ids_ref[...]) - lax.broadcasted_iota(jnp.int32, (HN, QD), 0) * PD
    for owner_z in range(NZ):
        ids_byz[owner_z] = turned[2 * owner_z : 2 * owner_z + 2, :]
    ids_in[0] = ids_byz[z]

    loads[0].wait()
    pl.semaphore_wait(barrier, len(peers))

    def ag(direction, n):
        hops = n // 2
        rows = pl.ds((direction if n % 2 == 0 else 1 - direction) * SUB, SUB)
        return remote(
            qbuf.at[slot_of(direction, hops), rows],
            qbuf.at[slot_of(direction, hops + 1), rows],
            ag_s.at[direction, n],
            ag_r.at[direction, n],
            at_z(1 if direction == 0 else -1),
        )

    def ag_send(n):
        for direction in (0, 1):
            ag(direction, n).start()

    def ag_arrive(n):
        for direction in (0, 1):
            ag(direction, n).wait_recv()
            if n + 2 <= 6:
                ag(direction, n + 2).start()

    ag_send(0)
    ag_send(1)

    def small(src, dst, which, slot):
        return remote(src, dst.at[MIRROR[slot]], one_s.at[which], one_r.at[which], at_z(slot_shift(slot)))

    def small_wait(buf, sem):
        pltpu.make_async_copy(buf.at[pl.ds(1, NZ - 1)], buf.at[pl.ds(1, NZ - 1)], sem).wait()

    for slot in range(1, NZ):
        small(ids_byz.at[(z + slot_shift(slot)) % NZ], ids_in, 0, slot).start()

    loads[1].wait()
    loads[2].wait()
    own_rows = pl.ds(pl.multiple_of(pa * IB, IB), IB)

    def batch_tile(i, carry):
        cols = pl.ds(pl.multiple_of(i * 256, 256), 256)
        column[own_rows, cols] = dot(bh[...], proj[:, cols]).astype(BF16)
        return carry

    lax.fori_loop(0, 4, batch_tile, 0)
    for shift in range(1, NY):
        remote(column.at[own_rows], column.at[own_rows], one_s.at[3], one_r.at[3], at_y(shift)).start()

    loads[3].wait()
    pool_rows = pl.ds(pl.multiple_of(core * PD, PD), PD)

    def pool_tile(i, carry):
        cols = pl.ds(pl.multiple_of(i * 256, 256), 256)
        pool[pool_rows, cols] = dot(ph[...], proj[:, cols]).astype(BF16)
        return carry

    lax.fori_loop(0, 4, pool_tile, 0)
    pool_swap = remote(pool.at[pool_rows], pool.at[pool_rows], one_s.at[5], one_r.at[5], partner)
    pool_swap.start()

    ag_arrive(0)

    lists_turned = lists_ref[...]
    high = (lists_turned // 32).astype(F32).astype(BF16)
    low = (lists_turned % 32).astype(F32).astype(BF16)
    one = eye(NG)
    high = dot_nt(one, high).astype(BF16)
    low = dot_nt(one, low).astype(BF16)
    in_group = lax.broadcasted_iota(jnp.int32, (NG, QD), 0) == group_ref[...]
    in_group = jnp.where(in_group, 1.0, 0.0).astype(BF16)
    chosen[...] = (dot(high, in_group) * 32.0 + dot(low, in_group)).astype(jnp.int32)
    at_label = lax.broadcasted_iota(jnp.int32, (GS, QD), 0) == label_ref[...]
    label_row = jnp.sum(jnp.where(at_label, chosen[...], 0), axis=0, keepdims=True)

    def mask_tile(i, carry):
        base = pl.multiple_of(i * 64, 64)
        row = lax.broadcasted_iota(jnp.int32, (64, QD), 0) + base
        found = jnp.zeros((64, QD), F32)
        for c in range(GS):
            found = jnp.where(row == chosen[c : c + 1, :], 1.0, found)
        mask[pl.ds(base, 64), :] = found
        return carry

    lax.fori_loop(0, NB // 64, mask_tile, 0)

    def slab(shift, half):
        start = ((x + shift + NX) % NX) * SLAB + half * (SLAB // 2)
        return pl.ds(pl.multiple_of(start, SLAB // 2), SLAB // 2)

    def xa(direction, n):
        half = direction if n % 2 == 0 else 1 - direction
        sign = 1 if direction == 0 else -1
        rows = slab(0 if n < 2 else -sign, half)
        return remote(column.at[rows], column.at[rows], xa_s.at[direction, n], xa_r.at[direction, n], at_x(sign))

    def y_wait(buf, sem):
        pltpu.make_async_copy(buf, buf, sem).wait()

    y_wait(column.at[pl.ds(0, (NY - 1) * IB)], one_r.at[3])
    for n in (0, 1):
        for direction in (0, 1):
            xa(direction, n).start()

    def xa_arrive(n):
        for direction in (0, 1):
            xa(direction, n).wait_recv()
            if n == 0:
                xa(direction, 2).start()

    def score(slot, count):
        queries = qbuf[slot : slot + count].reshape(count * QD, D)
        for k in (0, 1):

            def tile(i, carry):
                base = pl.multiple_of(i * 256, 256)
                rows = pl.ds(pl.multiple_of(k * PD + base, 256), 256)
                scores = dot_nt(pool[rows, :], queries)
                iota = lax.broadcasted_iota(jnp.int32, (256, QD), 0) + base
                new = []
                for j in range(count):
                    hit = iota == ids_in[slot + j, k : k + 1, :]
                    ot[rows, (slot + j) * QD : (slot + j + 1) * QD] = jnp.where(hit, 1.0, 0.0).astype(BF16)
                    found = jnp.where(hit, scores[:, j * QD : (j + 1) * QD], 0.0)
                    new.append(carry[j] + jnp.sum(found, axis=0, keepdims=True))
                return tuple(new)

            sums = lax.fori_loop(0, 2, tile, tuple(jnp.zeros((1, QD), F32) for _ in range(count)))
            for j in range(count):
                target = hs_in if slot == 0 else hs_out
                target[slot + j, k : k + 1, :] = sums[j] * SCALE
        for j in range(count):
            if slot > 0:
                small(hs_out.at[slot + j], hs_in, 1, slot + j).start()

    ag_arrive(1)
    small_wait(ids_in, one_r.at[0])
    pool_swap.wait_recv()
    score(0, 1)
    ag_arrive(2)
    score(1, 2)
    xa_arrive(0)
    ag_arrive(3)
    score(3, 2)
    for slot in range(NZ):
        rows16[2 * slot : 2 * slot + 2, :] = ids_in[slot].astype(F32)
    idcol[...] = turn_rows(rows16[...])
    ag_arrive(4)
    ag_arrive(5)
    score(5, 2)
    xa_arrive(1)
    xa_arrive(2)

    def dense_tile(i, carry):
        rows = pl.ds(pl.multiple_of(i * 256, 256), 256)
        value = dot_nt(column[rows, :], qbuf[0]) * SCALE
        dense[rows, :] = jnp.where(mask[rows, :] > 0.0, value, LOW)
        return carry

    lax.fori_loop(0, NB // 256, dense_tile, 0)
    group_max = jnp.max(dense[...], axis=0, keepdims=True)
    ag_arrive(6)
    score(7, 1)

    small_wait(hs_in, one_r.at[1])
    hard = hs_in[...]
    top = jnp.maximum(group_max, jnp.max(jnp.max(hard, axis=0), axis=0, keepdims=True))
    hard = jnp.exp(hard - top[None])
    likely = jnp.where(mask[...] > 0.0, jnp.exp(dense[...] - top), 0.0)
    total = jnp.sum(likely, axis=0, keepdims=True) + jnp.sum(jnp.sum(hard, axis=0), axis=0, keepdims=True)
    d_hard = (hard / total[None]).astype(BF16).astype(F32)
    d_out[...] = d_hard
    d_in[0] = d_hard[0]
    for slot in range(1, NZ):
        small(d_out.at[slot], d_in, 2, slot).start()
    target = jnp.where(lax.broadcasted_iota(jnp.int32, (NB, QD), 0) == label_row, 1.0, 0.0)
    dg[...] = (likely / total - target).astype(BF16)

    def part_tile(i, carry):
        cols = pl.ds(pl.multiple_of(i * 256, 256), 256)
        part[:, cols] = dot(dg[...], qbuf[0, :, cols]) * SCALE
        return carry

    lax.fori_loop(0, 4, part_tile, 0)

    def xr(direction, n):
        return remote(
            xr_out.at[direction, n],
            xr_in.at[direction, n],
            xr_s.at[direction, n],
            xr_r.at[direction, n],
            at_x(1 if direction == 0 else -1),
        )

    def xr_send(n):
        for direction in (0, 1):
            half = direction if n % 2 == 0 else 1 - direction
            sign = 1 if direction == 0 else -1
            value = part[slab(2 if n == 0 else sign, half), :]
            if n == 2:
                xr(direction, 0).wait_recv()
                value = value + xr_in[direction, 0].astype(F32)
            xr_out[direction, n] = value.astype(BF16)
            xr(direction, n).start()

    xr_send(0)
    xr_send(1)

    def rs(direction, n):
        return remote(
            rs_out.at[direction, n],
            rs_in.at[direction, n],
            rs_s.at[direction, n],
            rs_r.at[direction, n],
            at_z(1 if direction == 0 else -1),
        )

    def rs_send(n):
        hops = 4 - (n + 1) // 2
        for direction in (0, 1):
            half = direction if n % 2 == 0 else 1 - direction
            value = t_buf[slot_of(1 - direction, hops), half * SUB : (half + 1) * SUB, :]
            if n >= 2:
                rs(direction, n - 2).wait_recv()
                value = value + rs_in[direction, n - 2].astype(F32)
            rs_out[direction, n] = value.astype(BF16)
            rs(direction, n).start()

    def terms(slot, count):
        lane = lax.broadcasted_iota(jnp.int32, (QD, PD), 1)
        for j in range(count):
            for k in (0, 1):
                at = 2 * (slot + j) + k
                hit = lane == idcol[:, at : at + 1]
                value = jnp.where(hit, dcol[:, at : at + 1], 0.0)
                o_buf[j * QD : (j + 1) * QD, k * PD : (k + 1) * PD] = value.astype(BF16)

        def tile(i, carry):
            cols = pl.ds(pl.multiple_of(i * 256, 256), 256)
            value = dot(o_buf[0 : count * QD, :], pool[:, cols])
            for j in range(count):
                t_buf[slot + j, :, cols] = value[j * QD : (j + 1) * QD]
            return carry

        lax.fori_loop(0, 4, tile, 0)

    small_wait(d_in, one_r.at[2])
    for slot in range(NZ):
        rows16[2 * slot : 2 * slot + 2, :] = d_in[slot]
    dcol[...] = dot_nt(eye(QD), rows16[...].astype(BF16))
    terms(7, 1)
    rs_send(0)
    terms(5, 2)
    rs_send(1)

    dg_turned = dot_nt(eye(QD), dg[...]).astype(BF16)

    def group_tile(i, carry):
        cols = pl.ds(pl.multiple_of(i * 256, 256), 256)
        gterm[:, cols] = dot(dg_turned, column[:, cols])
        return carry

    lax.fori_loop(0, 4, group_tile, 0)
    xr_send(2)
    terms(3, 2)
    rs_send(2)
    terms(1, 2)
    terms(0, 1)
    rs_send(3)

    def contribs(k):
        for slot in range(NZ):
            at = 2 * slot
            weight = jnp.where(k == 0, dcol[:, at : at + 1], dcol[:, at + 1 : at + 2]) * SCALE
            contrib[slot * QD : (slot + 1) * QD, :] = (qbuf[slot].astype(F32) * weight).astype(BF16)

    def pool_sum(k, target, first, last):
        def tile(i, carry):
            cols = pl.ds(pl.multiple_of(i * 256, 256), 256)
            target[:, cols] = dot(ot[pl.ds(pl.multiple_of(k * PD, PD), PD), :], contrib[:, cols])
            return carry

        lax.fori_loop(first, last, tile, 0)

    contribs(1 - core)
    rs_send(4)
    pool_sum(1 - core, g_send, 0, 4)
    g_swap = remote(g_send, g_recv, one_s.at[6], one_r.at[6], partner)
    g_swap.start()
    rs_send(5)

    for direction in (0, 1):
        xr(direction, 1).wait_recv()
        xr(direction, 2).wait_recv()
    for half in (0, 1):
        value = part[slab(0, half), :]
        value = value + xr_in[half, 2].astype(F32) + xr_in[1 - half, 1].astype(F32)
        xsum[half * 4 : half * 4 + 4] = value.reshape(NY // 2, IB, D)
        y_out[half * 4 : half * 4 + 4] = value.astype(BF16).reshape(NY // 2, IB, D)
    for shift in range(1, NY):
        remote(
            y_out.at[(y + shift) % NY], y_in.at[shift], one_s.at[4], one_r.at[4], at_y(shift)
        ).start()
    contribs(core)
    rs_send(6)
    pool_sum(core, g_own, 0, 4)
    g_swap.wait_recv()
    gb[...] = (g_own[...] + g_recv[...]).astype(BF16)

    def pool_out(i, carry):
        cols = pl.ds(pl.multiple_of(i * 256, 256), 256)
        pg_stage[:, cols] = dot_nt(gb[...], proj[cols, :]).astype(BF16)
        return carry

    lax.fori_loop(0, 4, pool_out, 0)
    pg_store = pltpu.make_async_copy(pg_stage, pg_out, st_sem.at[0])
    pg_store.start()

    y_wait(y_in.at[pl.ds(1, NY - 1)], one_r.at[4])
    value = xsum[y]
    for shift in range(1, NY):
        value = value + y_in[shift].astype(F32)
    value = value.astype(BF16)

    def batch_out(i, carry):
        cols = pl.ds(pl.multiple_of(i * 256, 256), 256)
        bg_stage[:, cols] = dot_nt(value, proj[cols, :]).astype(BF16)
        return carry

    lax.fori_loop(0, 4, batch_out, 0)
    bg_store = pltpu.make_async_copy(bg_stage, bg_out, st_sem.at[1])
    bg_store.start()

    for direction in (0, 1):
        rs(direction, 5).wait_recv()
        rs(direction, 6).wait_recv()
    for half in (0, 1):
        rows = slice(half * SUB, (half + 1) * SUB)
        value = gterm[rows, :] + t_buf[0, rows, :]
        value = value + (rs_in[half, 6].astype(F32) + rs_in[1 - half, 5].astype(F32))
        qg_stage[rows, :] = (value * SCALE).astype(BF16)
    qg_store = pltpu.make_async_copy(qg_stage, qg_out, st_sem.at[2])
    qg_store.start()

    for direction in (0, 1):
        for n in range(7):
            ag(direction, n).wait_send()
            rs(direction, n).wait_send()
        for n in range(3):
            xa(direction, n).wait_send()
            xr(direction, n).wait_send()
    small_wait(ids_in, one_s.at[0])
    small_wait(hs_in, one_s.at[1])
    small_wait(d_in, one_s.at[2])
    y_wait(column.at[pl.ds(0, (NY - 1) * IB)], one_s.at[3])
    y_wait(y_in.at[pl.ds(1, NY - 1)], one_s.at[4])
    pool_swap.wait_send()
    g_swap.wait_send()
    pg_store.wait()
    bg_store.wait()
    qg_store.wait()


def turn_rows(rows):
    high = jnp.floor(rows * (1.0 / 32.0))
    low = rows - high * 32.0
    one = eye(QD)
    turned = dot_nt(one, high.astype(BF16)) * 32.0 + dot_nt(one, low.astype(BF16))
    return turned.astype(jnp.int32)


def shards(queries, batch_hidden, pool_hidden, projection, hard_ids, query_group, labels, group_lists):
    hbm = pl.BlockSpec(memory_space=pl.ANY)
    vmem = pl.BlockSpec(memory_space=pltpu.VMEM)
    dma = pltpu.SemaphoreType.DMA
    scratch = [
        pltpu.VMEM((NZ, QD, D), BF16),
        pltpu.VMEM((D, D), BF16),
        pltpu.VMEM((IB, D), BF16),
        pltpu.VMEM((PD, D), BF16),
        pltpu.VMEM((2 * PD, D), BF16),
        pltpu.VMEM((NB, D), BF16),
        pltpu.VMEM((2 * PD, NZ * QD), BF16),
        pltpu.VMEM((NB, QD), F32),
        pltpu.VMEM((NB, QD), F32),
        pltpu.VMEM((GS, QD), jnp.int32),
        pltpu.VMEM((NZ, 2, QD), jnp.int32),
        pltpu.VMEM((NZ, 2, QD), jnp.int32),
        pltpu.VMEM((NZ, 2, QD), F32),
        pltpu.VMEM((NZ, 2, QD), F32),
        pltpu.VMEM((NZ, 2, QD), F32),
        pltpu.VMEM((NZ, 2, QD), F32),
        pltpu.VMEM((HN, QD), F32),
        pltpu.VMEM((QD, HN), jnp.int32),
        pltpu.VMEM((QD, HN), F32),
        pltpu.VMEM((NZ, QD, D), F32),
        pltpu.VMEM((2 * QD, 2 * PD), BF16),
        pltpu.VMEM((2, 7, SUB, D), BF16),
        pltpu.VMEM((2, 7, SUB, D), BF16),
        pltpu.VMEM((NB, QD), BF16),
        pltpu.VMEM((NB, D), F32),
        pltpu.VMEM((2, 3, SLAB // 2, D), BF16),
        pltpu.VMEM((2, 3, SLAB // 2, D), BF16),
        pltpu.VMEM((NY, IB, D), F32),
        pltpu.VMEM((NY, IB, D), BF16),
        pltpu.VMEM((NY, IB, D), BF16),
        pltpu.VMEM((QD, D), F32),
        pltpu.VMEM((NZ * QD, D), BF16),
        pltpu.VMEM((PD, D), F32),
        pltpu.VMEM((PD, D), F32),
        pltpu.VMEM((PD, D), F32),
        pltpu.VMEM((PD, D), BF16),
        pltpu.VMEM((QD, D), BF16),
        pltpu.VMEM((IB, D), BF16),
        pltpu.VMEM((PD, D), BF16),
        dma((4,)),
        dma((3,)),
        dma((2, 7)),
        dma((2, 7)),
        dma((2, 7)),
        dma((2, 7)),
        dma((2, 3)),
        dma((2, 3)),
        dma((2, 3)),
        dma((2, 3)),
        dma((7,)),
        dma((7,)),
    ]
    return pl.pallas_call(
        kernel,
        out_shape=(
            jax.ShapeDtypeStruct((QD, D), BF16),
            jax.ShapeDtypeStruct((IB, D), BF16),
            jax.ShapeDtypeStruct((PD, D), BF16),
        ),
        in_specs=[hbm] * 4 + [vmem] * 4,
        out_specs=(hbm, hbm, hbm),
        scratch_shapes=scratch,
        compiler_params=pltpu.CompilerParams(
            collective_id=0, has_side_effects=True, vmem_limit_bytes=56 * 1024 * 1024
        ),
        cost_estimate=pl.CostEstimate(flops=9_000_000_000, bytes_accessed=6_000_000, transcendentals=100_000),
    )(
        queries, batch_hidden, pool_hidden, projection, hard_ids,
        query_group.reshape(1, QD), labels.reshape(1, QD), group_lists,
    )


def solution(mesh):
    return jax.shard_map(
        shards,
        mesh=mesh,
        in_specs=(
            P(("pa", "pb"), None),
            P(("pa", "pb"), None),
            P(("pa", "pb"), None),
            P(),
            P(("pa", "pb"), None),
            P(("pa", "pb")),
            P(("pa", "pb")),
            P(),
        ),
        out_specs=(P(("pa", "pb"), None), P(("pa", "pb"), None), P(("pa", "pb"), None)),
        check_vma=False,
    )
```

time: 426 us -> 80 us (0.19)
  waiting for transfers between devices: 330 us -> 0 us
  Pallas kernels: 0 us -> 72.2 us
  matrix products: 26 us -> 0 us
  other arithmetic: 22.9 us -> 0 us
  starting transfers between devices: 19.7 us -> 0 us
  between operations: 13.9 us -> 0.64 us
  blocking collectives: 10.4 us -> 0 us
  local copies, waits for them, and re-layouts: 2.04 us -> 6.73 us
    reduce_scatter x1 -> x0, waiting for transfers between devices: 215 us -> none  [shards(): lax.psum_scatter(batch_part, 'pa', scatter_dimension=0, tiled=True)]
    all_gather x2 -> x0, waiting for transfers between devices: 105 us -> none  [the longest x1 59.4 us: shards(): column = lax.all_gather(batch_proj, 'pa', axis=0, tiled=True)]
    pallas_call x0 -> x1, Pallas kernels: none -> 72.2 us  [shards(): pl.pallas_call(kernel, out_shape=(jax.ShapeDtypeStruct((QD, D), BF16), ja...]
    dot_general x8 -> x0, matrix products: 26 us -> none  [the longest x1 6.71 us: shards(): lax.dot_general(pool_grad.astype(jnp.bfloat16), projection, dims, preferr...]
    all_to_all x3 -> x0, starting transfers between devices: 19.4 us -> none  [the longest x1 10.4 us: shards(): lax.all_to_all(requests, 'pb', split_axis=0, concat_axis=0, tiled=True)]
    dot_general x2 -> x0, other arithmetic: 10.6 us -> none  [the longest x1 6.01 us: shards(): jnp.einsum('sij,sijd->sid', sent_back, picked, preferred_element_type=jnp...]
    all_to_all x1 -> x0, blocking collectives: 10.4 us -> none  [shards(): lax.all_to_all(grad_hard, 'pb', split_axis=0, concat_axis=0, tiled=True)]
    all_to_all x3 -> x0, waiting for transfers between devices: 10.2 us -> none  [the longest x1 5.97 us: shards(): lax.all_to_all(requests, 'pb', split_axis=0, concat_axis=0, tiled=True)]
  transfers between devices with their start and end apart: 6 -> 0, of which waited for: 5 -> 0; matrix products, arithmetic and copies ran while one was open for 7% -> 0% of each run, Pallas kernels for 0% -> 0%
where the time goes in v1:
time: 80 us; the launch traced here: 79.6 us
  Pallas kernels  72.2 us (90%)
  local copies, waits for them, and re-layouts  6.73 us (8%)
    pallas_call x1, Pallas kernels, shards(): pl.pallas_call(kernel, out_shape=(jax.ShapeDtypeStruct((QD, D), BF16), ja...  72.2 us
    unnamed x4, local copies, waits for them, and re-layouts  6.73 us

profile of v1, /device:TPU:6, one launch (start us, length us, event | category | flops | bytes accessed | tf_op | source)
XLA Modules:
  0.0 79.6 jit_solution(12516084769397465304)
XLA Ops:
  0.6 1.4 %copy.11.ids_ref = s32[128,16]{1,0:T(8,128)} copy(s32[128,16]{0,1:T(8,128)} %param.12) | data formatting | bytes 16384 | tf_op args[4]
  2.1 72.2 %shard_map.103 = (bf16[128,1024]{1,0:T(8,128)(2,1)}, bf16[16,1024]{1,0:T(8,128)(2,1)}, bf16[512,1024]{1,0:T(8,128)(2,1)}) custom-call(bf16[128,1024]{1,0:T(8,128)(2,1)} %q_hbm.1, bf16[16,1024]{1,0:T(8,128)(2,1)} %bh_hbm.1, bf16[512,1024]{1,0:T(8,128)(2,1)} %ph_hbm.1, bf16[1024,1024]{1,0:T(8,128)(2,1)} %proj_hbm.1, s32[128,16]{1,0:T(8,128)} %copy.11.ids_ref, ...), custom_call_target="tpu_custom_call" | custom-call | flops 8999999488 | bytes 6000000 | tf_op jit(solution)/shard_map/pallas_call | solution.py:542
  74.3 1.7 %copy.15 = bf16[128,1024]{1,0:T(8,128)(2,1)} copy(bf16[128,1024]{1,0:T(8,128)(2,1)} %get-tuple-element.6) | data formatting | bytes 524288
  76.0 1.4 %copy.16 = bf16[16,1024]{1,0:T(8,128)(2,1)} copy(bf16[16,1024]{1,0:T(8,128)(2,1)} %get-tuple-element.7) | data formatting | bytes 65536
  77.3 2.3 %copy.17 = bf16[512,1024]{1,0:T(8,128)(2,1)} copy(bf16[512,1024]{1,0:T(8,128)(2,1)} %get-tuple-element.8) | data formatting | bytes 2097152

commit v2 on v1

v2 whole, which is shorter than its diff:
```python
import math

import jax
import jax.numpy as jnp
from jax import lax
from jax.experimental import pallas as pl
from jax.experimental.pallas import tpu as pltpu
from jax.sharding import PartitionSpec as P

MESH = pl.DeviceIdType.MESH
NX, NY, NZ = 4, 8, 8
D = 1024
QD = 128
PD = 512
IB = 16
NG = 64
GS = 64
HN = 16
NB = NX * NY * IB
SLAB = NY * IB
SUB = QD // 2
HD = D // 2
SCALE = 1.0 / math.sqrt(D)
F32 = jnp.float32
BF16 = jnp.bfloat16
LOW = -3.0e38

MIRROR = (0, 1, 3, 2, 5, 4, 7, 6)


def slot_of(direction, hops):
    if hops == 0:
        return 0
    if hops == 4:
        return 1
    return 2 * hops + direction


def slot_shift(slot):
    if slot < 2:
        return 4 * slot
    hops = slot // 2
    return (hops if slot % 2 else -hops) % NZ


def dot(a, b):
    return jnp.dot(a, b, preferred_element_type=F32)


def dot_nt(a, b):
    return lax.dot_general(a, b, (((1,), (1,)), ((), ())), preferred_element_type=F32)


def eye(n):
    same = lax.broadcasted_iota(jnp.int32, (n, n), 0) == lax.broadcasted_iota(jnp.int32, (n, n), 1)
    return jnp.where(same, 1.0, 0.0).astype(BF16)


def turn_rows(rows):
    high = jnp.floor(rows * (1.0 / 32.0))
    low = rows - high * 32.0
    one = eye(QD)
    turned = dot_nt(one, high.astype(BF16)) * 32.0 + dot_nt(one, low.astype(BF16))
    return turned.astype(jnp.int32)


def kernel(
    q_hbm, bh_hbm, ph_hbm, proj_hbm, ids_ref, group_ref, label_ref, lists_ref,
    qg_out, bg_out, pg_out,
    qbuf, proj, bh, ph, pool, column, ot, mask, dense, chosen,
    ids_byz, ids_in, hs_out, hs_in, d_out, d_in, rows16, idcol, dcol,
    t_buf, o_buf, rs_out, rs_in, dg, part, xr_out, xr_in, xsum, y_out, y_in, gterm,
    contrib, g_send, g_recv, g_own, gb,
    ld_sem, ag_s, ag_r, rs_s, rs_r, xa_s, xa_r, xr_s, xr_r, one_s, one_r, z_ready, xy_ready,
):
    pa = lax.axis_index("pa")
    pb = lax.axis_index("pb")
    x, y = pa // NY, pa % NY
    z, core = pb // 2, pb % 2

    def at_z(shift):
        return (pa, ((z + shift + NZ) % NZ) * 2 + core)

    def at_y(shift):
        return (x * NY + (y + shift) % NY, pb)

    def at_x(shift):
        return (((x + shift + NX) % NX) * NY + y, pb)

    partner = (pa, z * 2 + 1 - core)

    def remote(src, dst, send, recv, device):
        return pltpu.make_async_remote_copy(
            src_ref=src, dst_ref=dst, send_sem=send, recv_sem=recv, device_id=device, device_id_type=MESH
        )

    barrier = pltpu.get_barrier_semaphore()

    def hello(device):
        pl.semaphore_signal(barrier, inc=1, device_id=device, device_id_type=MESH)

    for shift in range(1, NZ):
        hello((pa, ((z + shift) % NZ) * 2))
    hello(partner)
    for shift in range(1, NY):
        hello((x * NY + (y + shift) % NY, z * 2 + 1))
    for shift in (1, NX - 1):
        hello((((x + shift) % NX) * NY + y, z * 2 + 1))

    loads = [
        pltpu.make_async_copy(q_hbm, qbuf.at[0], ld_sem.at[0]),
        pltpu.make_async_copy(bh_hbm, bh, ld_sem.at[1]),
        pltpu.make_async_copy(proj_hbm, proj, ld_sem.at[2]),
        pltpu.make_async_copy(ph_hbm, ph, ld_sem.at[3]),
    ]
    for load in loads:
        load.start()
    loads[0].wait()

    @pl.when(core == 0)
    def _():
        pl.semaphore_wait(barrier, 2 * (NZ - 1) + 1)
        pl.semaphore_signal(z_ready, inc=1, device_id=partner, device_id_type=MESH)

    @pl.when(core == 1)
    def _():
        pl.semaphore_wait(z_ready, 1)

    def ag(direction, n):
        hops = n // 2
        rows = pl.ds((direction if n % 2 == 0 else 1 - direction) * SUB, SUB)
        return remote(
            qbuf.at[slot_of(direction, hops), rows],
            qbuf.at[slot_of(direction, hops + 1), rows],
            ag_s.at[direction, n],
            ag_r.at[direction, n],
            at_z(1 if direction == 0 else -1),
        )

    def ag_arrive(n):
        for direction in (0, 1):
            ag(direction, n).wait_recv()
            if n + 2 <= 6:
                ag(direction, n + 2).start()

    for n in (0, 1):
        for direction in (0, 1):
            ag(direction, n).start()

    def small(src, dst, which, slot):
        return remote(src, dst.at[MIRROR[slot]], one_s.at[which], one_r.at[which], at_z(slot_shift(slot)))

    def small_wait(buf, sem):
        pltpu.make_async_copy(buf.at[pl.ds(1, NZ - 1)], buf.at[pl.ds(1, NZ - 1)], sem).wait()

    loads[1].wait()
    loads[2].wait()
    own_rows = pl.ds(pl.multiple_of(pa * IB, IB), IB)

    def batch_half(half):
        def tile(i, carry):
            cols = pl.ds(pl.multiple_of(i * 256, 256), 256)
            wide = pl.ds(pl.multiple_of(half * HD + i * 256, 256), 256)
            column[half, own_rows, cols] = dot(bh[...], proj[:, wide]).astype(BF16)
            return carry

        lax.fori_loop(0, 2, tile, 0)

    def ya_send(half):
        here = column.at[half, own_rows]
        for shift in range(1, NY):
            remote(here, here, one_s.at[9 + half], one_r.at[9 + half], at_y(shift)).start()

    batch_half(0)

    @pl.when(core == 1)
    def _():
        pl.semaphore_wait(barrier, 2 * (NY - 1) + 2 * 2 + 1)
        pl.semaphore_signal(xy_ready, inc=1, device_id=partner, device_id_type=MESH)

    @pl.when(core == 0)
    def _():
        pl.semaphore_wait(xy_ready, 1)

    ya_send(0)
    batch_half(1)
    ya_send(1)

    local_rows = ids_ref[...] - lax.broadcasted_iota(jnp.int32, (HN, QD), 0) * PD
    for owner_z in range(NZ):
        ids_byz[owner_z] = local_rows[2 * owner_z : 2 * owner_z + 2, :]
    ids_in[0] = ids_byz[z]
    for slot in range(1, NZ):
        small(ids_byz.at[(z + slot_shift(slot)) % NZ], ids_in, 0, slot).start()

    ag_arrive(0)
    loads[3].wait()
    pool_rows = pl.ds(pl.multiple_of(core * PD, PD), PD)

    def pool_tile(i, carry):
        cols = pl.ds(pl.multiple_of(i * 256, 256), 256)
        pool[pool_rows, cols] = dot(ph[...], proj[:, cols]).astype(BF16)
        return carry

    lax.fori_loop(0, 4, pool_tile, 0)
    pool_swap = remote(pool.at[pool_rows], pool.at[pool_rows], one_s.at[7], one_r.at[7], partner)
    pool_swap.start()
    ag_arrive(1)

    lists_turned = lists_ref[...]
    high = (lists_turned // 32).astype(F32).astype(BF16)
    low = (lists_turned % 32).astype(F32).astype(BF16)
    one = eye(NG)
    high = dot_nt(one, high).astype(BF16)
    low = dot_nt(one, low).astype(BF16)
    in_group = lax.broadcasted_iota(jnp.int32, (NG, QD), 0) == group_ref[...]
    in_group = jnp.where(in_group, 1.0, 0.0).astype(BF16)
    chosen[...] = (dot(high, in_group) * 32.0 + dot(low, in_group)).astype(jnp.int32)
    at_label = lax.broadcasted_iota(jnp.int32, (GS, QD), 0) == label_ref[...]
    label_row = jnp.sum(jnp.where(at_label, chosen[...], 0), axis=0, keepdims=True)

    def mask_tile(i, carry):
        base = pl.multiple_of(i * 64, 64)
        row = lax.broadcasted_iota(jnp.int32, (64, QD), 0) + base
        found = jnp.zeros((64, QD), F32)
        for c in range(GS):
            found = jnp.where(row == chosen[c : c + 1, :], 1.0, found)
        mask[pl.ds(base, 64), :] = found
        return carry

    def slab(shift, half):
        start = ((x + shift + NX) % NX) * SLAB + half * (SLAB // 2)
        return pl.ds(pl.multiple_of(start, SLAB // 2), SLAB // 2)

    def xa(part_of, direction, n):
        half = direction if n % 2 == 0 else 1 - direction
        sign = 1 if direction == 0 else -1
        here = column.at[part_of, slab(0 if n < 2 else -sign, half)]
        return remote(here, here, xa_s.at[part_of, direction, n], xa_r.at[part_of, direction, n], at_x(sign))

    def all_wait(buf, sem):
        pltpu.make_async_copy(buf, buf, sem).wait()

    def xa_send(part_of):
        all_wait(column.at[part_of, pl.ds(0, (NY - 1) * IB)], one_r.at[9 + part_of])
        for n in (0, 1):
            for direction in (0, 1):
                xa(part_of, direction, n).start()

    def xa_arrive(part_of, n):
        for direction in (0, 1):
            xa(part_of, direction, n).wait_recv()
            if n == 0:
                xa(part_of, direction, 2).start()

    xa_send(0)
    lax.fori_loop(0, NB // 128, mask_tile, 0)
    ag_arrive(2)
    xa_send(1)
    small_wait(ids_in, one_r.at[0])
    for slot in range(NZ):
        rows16[2 * slot : 2 * slot + 2, :] = ids_in[slot].astype(F32)
    idcol[...] = turn_rows(rows16[...])
    pool_swap.wait_recv()

    def score(slot):
        queries = qbuf[slot : slot + 2].reshape(2 * QD, D)
        for k in (0, 1):

            def tile(i, carry):
                base = pl.multiple_of(i * 256, 256)
                rows = pl.ds(pl.multiple_of(k * PD + base, 256), 256)
                scores = dot_nt(pool[rows, :], queries)
                iota = lax.broadcasted_iota(jnp.int32, (256, QD), 0) + base
                new = []
                for j in (0, 1):
                    hit = iota == ids_in[slot + j, k : k + 1, :]
                    ot[rows, (slot + j) * QD : (slot + j + 1) * QD] = jnp.where(hit, 1.0, 0.0).astype(BF16)
                    found = jnp.where(hit, scores[:, j * QD : (j + 1) * QD], 0.0)
                    new.append(carry[j] + jnp.sum(found, axis=0, keepdims=True))
                return tuple(new)

            sums = lax.fori_loop(0, 2, tile, tuple(jnp.zeros((1, QD), F32) for _ in (0, 1)))
            for j in (0, 1):
                target = hs_in if slot + j == 0 else hs_out
                target[slot + j, k : k + 1, :] = sums[j] * SCALE
        for j in (0, 1):
            if slot + j > 0:
                small(hs_out.at[slot + j], hs_in, 1, slot + j).start()

    def dense_half(half):
        def tile(i, carry):
            rows = pl.ds(pl.multiple_of(i * 256, 256), 256)
            value = dot_nt(column[half, rows, :], qbuf[0, :, half * HD : (half + 1) * HD])
            if half == 0:
                dense[rows, :] = value
            else:
                value = (dense[rows, :] + value) * SCALE
                dense[rows, :] = jnp.where(mask[rows, :] > 0.0, value, LOW)
            return carry

        lax.fori_loop(0, NB // 256, tile, 0)

    score(2)
    ag_arrive(3)
    xa_arrive(0, 0)
    score(4)
    ag_arrive(4)
    lax.fori_loop(NB // 128, NB // 64, mask_tile, 0)
    xa_arrive(1, 0)
    ag_arrive(5)
    score(6)
    xa_arrive(0, 1)
    xa_arrive(0, 2)
    dense_half(0)
    ag_arrive(6)
    score(0)
    xa_arrive(1, 1)
    xa_arrive(1, 2)
    dense_half(1)

    group_max = jnp.max(dense[...], axis=0, keepdims=True)
    small_wait(hs_in, one_r.at[1])
    hard = hs_in[...]
    top = jnp.maximum(group_max, jnp.max(jnp.max(hard, axis=0), axis=0, keepdims=True))
    hard = jnp.exp(hard - top[None])
    likely = jnp.where(mask[...] > 0.0, jnp.exp(dense[...] - top), 0.0)
    total = jnp.sum(likely, axis=0, keepdims=True) + jnp.sum(jnp.sum(hard, axis=0), axis=0, keepdims=True)
    d_hard = (hard / total[None]).astype(BF16).astype(F32)
    d_out[...] = d_hard
    d_in[0] = d_hard[0]
    for slot in range(1, NZ):
        small(d_out.at[slot], d_in, 3, slot).start()
    target = jnp.where(lax.broadcasted_iota(jnp.int32, (NB, QD), 0) == label_row, 1.0, 0.0)
    dg[...] = (likely / total - target).astype(BF16)

    def rs(direction, n):
        return remote(
            rs_out.at[direction, n],
            rs_in.at[direction, n],
            rs_s.at[direction, n],
            rs_r.at[direction, n],
            at_z(1 if direction == 0 else -1),
        )

    def rs_send(n):
        hops = 4 - (n + 1) // 2
        for direction in (0, 1):
            half = direction if n % 2 == 0 else 1 - direction
            value = t_buf[slot_of(1 - direction, hops), half * SUB : (half + 1) * SUB, :]
            if n >= 2:
                rs(direction, n - 2).wait_recv()
                value = value + rs_in[direction, n - 2].astype(F32)
            rs_out[direction, n] = value.astype(BF16)
            rs(direction, n).start()

    def terms(slot):
        lane = lax.broadcasted_iota(jnp.int32, (QD, PD), 1)
        for j in (0, 1):
            for k in (0, 1):
                at = 2 * (slot + j) + k
                hit = lane == idcol[:, at : at + 1]
                value = jnp.where(hit, dcol[:, at : at + 1], 0.0)
                o_buf[j * QD : (j + 1) * QD, k * PD : (k + 1) * PD] = value.astype(BF16)

        def tile(i, carry):
            cols = pl.ds(pl.multiple_of(i * 256, 256), 256)
            value = dot(o_buf[...], pool[:, cols])
            t_buf[slot, :, cols] = value[0:QD]
            t_buf[slot + 1, :, cols] = value[QD : 2 * QD]
            return carry

        lax.fori_loop(0, 4, tile, 0)

    def part_half(half):
        def tile(i, carry):
            cols = pl.ds(pl.multiple_of(i * 256, 256), 256)
            wide = pl.ds(pl.multiple_of(half * HD + i * 256, 256), 256)
            part[half, :, cols] = dot(dg[...], qbuf[0, :, wide]) * SCALE
            return carry

        lax.fori_loop(0, 2, tile, 0)

    def xr(part_of, direction, n):
        return remote(
            xr_out.at[part_of, direction, n],
            xr_in.at[part_of, direction, n],
            xr_s.at[part_of, direction, n],
            xr_r.at[part_of, direction, n],
            at_x(1 if direction == 0 else -1),
        )

    def xr_send(part_of, n):
        for direction in (0, 1):
            half = direction if n % 2 == 0 else 1 - direction
            sign = 1 if direction == 0 else -1
            value = part[part_of, slab(2 if n == 0 else sign, half), :]
            if n == 2:
                xr(part_of, direction, 0).wait_recv()
                value = value + xr_in[part_of, direction, 0].astype(F32)
            xr_out[part_of, direction, n] = value.astype(BF16)
            xr(part_of, direction, n).start()

    def yr_send(part_of):
        for direction in (0, 1):
            xr(part_of, direction, 1).wait_recv()
            xr(part_of, direction, 2).wait_recv()
        for half in (0, 1):
            value = part[part_of, slab(0, half), :]
            value = value + xr_in[part_of, half, 2].astype(F32) + xr_in[part_of, 1 - half, 1].astype(F32)
            xsum[part_of, half * 4 : half * 4 + 4] = value.reshape(NY // 2, IB, HD)
            y_out[part_of, half * 4 : half * 4 + 4] = value.astype(BF16).reshape(NY // 2, IB, HD)
        for shift in range(1, NY):
            remote(
                y_out.at[part_of, (y + shift) % NY],
                y_in.at[part_of, shift],
                one_s.at[5 + part_of],
                one_r.at[5 + part_of],
                at_y(shift),
            ).start()

    def contribs(which):
        k = 1 - core if which == 0 else core
        for slot in range(NZ):
            at = 2 * slot
            weight = jnp.where(k == 0, dcol[:, at : at + 1], dcol[:, at + 1 : at + 2]) * SCALE
            contrib[which, slot * QD : (slot + 1) * QD, :] = (qbuf[slot].astype(F32) * weight).astype(BF16)

    def pool_sum(which, target, first, last):
        k = 1 - core if which == 0 else core

        def tile(i, carry):
            cols = pl.ds(pl.multiple_of(i * 256, 256), 256)
            target[:, cols] = dot(ot[pl.ds(pl.multiple_of(k * PD, PD), PD), :], contrib[which, :, cols])
            return carry

        lax.fori_loop(first, last, tile, 0)

    def group_term():
        dg_turned = dot_nt(eye(QD), dg[...]).astype(BF16)
        for half in (0, 1):

            def tile(i, carry):
                cols = pl.ds(pl.multiple_of(i * 256, 256), 256)
                wide = pl.ds(pl.multiple_of(half * HD + i * 256, 256), 256)
                gterm[:, wide] = dot(dg_turned, column[half, :, cols])
                return carry

            lax.fori_loop(0, 2, tile, 0)

    part_half(0)
    xr_send(0, 0)
    xr_send(0, 1)
    part_half(1)
    xr_send(1, 0)
    xr_send(1, 1)
    small_wait(d_in, one_r.at[3])
    for slot in range(NZ):
        rows16[2 * slot : 2 * slot + 2, :] = d_in[slot]
    dcol[...] = dot_nt(eye(QD), rows16[...].astype(BF16))
    terms(0)
    rs_send(0)
    terms(6)
    rs_send(1)
    terms(4)
    rs_send(2)
    terms(2)
    xr_send(0, 2)
    rs_send(3)
    xr_send(1, 2)
    contribs(0)
    rs_send(4)
    pool_sum(0, g_send, 0, 4)
    g_swap = remote(g_send, g_recv, one_s.at[8], one_r.at[8], partner)
    g_swap.start()
    yr_send(0)
    rs_send(5)
    yr_send(1)
    rs_send(6)
    contribs(1)
    pool_sum(1, g_own, 0, 4)
    group_term()
    g_swap.wait_recv()
    gb[...] = (g_own[...] + g_recv[...]).astype(BF16)

    def pool_out(i, carry):
        cols = pl.ds(pl.multiple_of(i * 256, 256), 256)
        pg_out[:, cols] = dot_nt(gb[...], proj[cols, :]).astype(BF16)
        return carry

    lax.fori_loop(0, 4, pool_out, 0)

    batch_sum = []
    for half in (0, 1):
        all_wait(y_in.at[half, pl.ds(1, NY - 1)], one_r.at[5 + half])
        value = xsum[half, y]
        for shift in range(1, NY):
            value = value + y_in[half, shift].astype(F32)
        batch_sum.append(value.astype(BF16))

    def batch_out(i, carry):
        cols = pl.ds(pl.multiple_of(i * 256, 256), 256)
        value = dot_nt(batch_sum[0], proj[cols, 0:HD]) + dot_nt(batch_sum[1], proj[cols, HD:D])
        bg_out[:, cols] = value.astype(BF16)
        return carry

    lax.fori_loop(0, 4, batch_out, 0)

    for direction in (0, 1):
        rs(direction, 5).wait_recv()
        rs(direction, 6).wait_recv()
    for half in (0, 1):
        rows = slice(half * SUB, (half + 1) * SUB)
        value = gterm[rows, :] + t_buf[0, rows, :]
        value = value + (rs_in[half, 6].astype(F32) + rs_in[1 - half, 5].astype(F32))
        qg_out[rows, :] = (value * SCALE).astype(BF16)

    for direction in (0, 1):
        for n in range(7):
            ag(direction, n).wait_send()
            rs(direction, n).wait_send()
        for n in range(3):
            for half in (0, 1):
                xa(half, direction, n).wait_send()
                xr(half, direction, n).wait_send()
    small_wait(ids_in, one_s.at[0])
    small_wait(hs_in, one_s.at[1])
    small_wait(d_in, one_s.at[3])
    for half in (0, 1):
        all_wait(column.at[half, pl.ds(0, (NY - 1) * IB)], one_s.at[9 + half])
        all_wait(y_in.at[half, pl.ds(1, NY - 1)], one_s.at[5 + half])
    pool_swap.wait_send()
    g_swap.wait_send()


def shards(queries, batch_hidden, pool_hidden, projection, hard_ids, query_group, labels, group_lists):
    hbm = pl.BlockSpec(memory_space=pl.ANY)
    vmem = pl.BlockSpec(memory_space=pltpu.VMEM)
    dma = pltpu.SemaphoreType.DMA
    scratch = [
        pltpu.VMEM((NZ, QD, D), BF16),
        pltpu.VMEM((D, D), BF16),
        pltpu.VMEM((IB, D), BF16),
        pltpu.VMEM((PD, D), BF16),
        pltpu.VMEM((2 * PD, D), BF16),
        pltpu.VMEM((2, NB, HD), BF16),
        pltpu.VMEM((2 * PD, NZ * QD), BF16),
        pltpu.VMEM((NB, QD), F32),
        pltpu.VMEM((NB, QD), F32),
        pltpu.VMEM((GS, QD), jnp.int32),
        pltpu.VMEM((NZ, 2, QD), jnp.int32),
        pltpu.VMEM((NZ, 2, QD), jnp.int32),
        pltpu.VMEM((NZ, 2, QD), F32),
        pltpu.VMEM((NZ, 2, QD), F32),
        pltpu.VMEM((NZ, 2, QD), F32),
        pltpu.VMEM((NZ, 2, QD), F32),
        pltpu.VMEM((HN, QD), F32),
        pltpu.VMEM((QD, HN), jnp.int32),
        pltpu.VMEM((QD, HN), F32),
        pltpu.VMEM((NZ, QD, D), F32),
        pltpu.VMEM((2 * QD, 2 * PD), BF16),
        pltpu.VMEM((2, 7, SUB, D), BF16),
        pltpu.VMEM((2, 7, SUB, D), BF16),
        pltpu.VMEM((NB, QD), BF16),
        pltpu.VMEM((2, NB, HD), F32),
        pltpu.VMEM((2, 2, 3, SLAB // 2, HD), BF16),
        pltpu.VMEM((2, 2, 3, SLAB // 2, HD), BF16),
        pltpu.VMEM((2, NY, IB, HD), F32),
        pltpu.VMEM((2, NY, IB, HD), BF16),
        pltpu.VMEM((2, NY, IB, HD), BF16),
        pltpu.VMEM((QD, D), F32),
        pltpu.VMEM((2, NZ * QD, D), BF16),
        pltpu.VMEM((PD, D), F32),
        pltpu.VMEM((PD, D), F32),
        pltpu.VMEM((PD, D), F32),
        pltpu.VMEM((PD, D), BF16),
        dma((4,)),
        dma((2, 7)),
        dma((2, 7)),
        dma((2, 7)),
        dma((2, 7)),
        dma((2, 2, 3)),
        dma((2, 2, 3)),
        dma((2, 2, 3)),
        dma((2, 2, 3)),
        dma((11,)),
        dma((11,)),
        pltpu.SemaphoreType.REGULAR,
        pltpu.SemaphoreType.REGULAR,
    ]
    shapes = (
        pltpu.VMEM((QD, D), BF16),
        pltpu.VMEM((IB, D), BF16),
        pltpu.VMEM((PD, D), BF16),
    )
    return pl.pallas_call(
        kernel,
        out_shape=shapes,
        in_specs=[hbm] * 4 + [vmem] * 4,
        out_specs=(vmem, vmem, vmem),
        scratch_shapes=scratch,
        compiler_params=pltpu.CompilerParams(
            collective_id=0, has_side_effects=True, vmem_limit_bytes=58 * 1024 * 1024
        ),
        cost_estimate=pl.CostEstimate(flops=9_000_000_000, bytes_accessed=6_000_000, transcendentals=100_000),
    )(
        queries, batch_hidden, pool_hidden, projection, hard_ids.T,
        query_group.reshape(1, QD), labels.reshape(1, QD), group_lists,
    )


def solution(mesh):
    return jax.shard_map(
        shards,
        mesh=mesh,
        in_specs=(
            P(("pa", "pb"), None),
            P(("pa", "pb"), None),
            P(("pa", "pb"), None),
            P(),
            P(("pa", "pb"), None),
            P(("pa", "pb")),
            P(("pa", "pb")),
            P(),
        ),
        out_specs=(P(("pa", "pb"), None), P(("pa", "pb"), None), P(("pa", "pb"), None)),
        check_vma=False,
    )
```

time: 80 us -> 75.1 us (0.939)
  local copies, waits for them, and re-layouts: 6.73 us -> 2.29 us
    unnamed x4 -> x3, local copies, waits for them, and re-layouts: 6.73 us -> 2.29 us
where the time goes in v2:
time: 75.1 us; the launch traced here: 74.9 us
  Pallas kernels  71.9 us (96%)
  local copies, waits for them, and re-layouts  2.29 us (3%)
    pallas_call x1, Pallas kernels, shards(): pl.pallas_call(kernel, out_shape=shapes, in_specs=[hbm] * 4 + [vmem] * 4,...  71.9 us
    unnamed x3, local copies, waits for them, and re-layouts  2.29 us

profile of v2, /device:TPU:6, one launch (start us, length us, event | category | flops | bytes accessed | tf_op | source)
XLA Modules:
  0.0 74.9 jit_solution(17995959831392543850)
XLA Ops:
  0.6 71.9 %shard_map.103 = (bf16[128,1024]{1,0:T(8,128)(2,1)S(1)}, bf16[16,1024]{1,0:T(8,128)(2,1)S(1)}, bf16[512,1024]{1,0:T(8,128)(2,1)S(1)}) custom-call(bf16[128,1024]{1,0:T(8,128)(2,1)} %q_hbm.1, bf16[16,1024]{1,0:T(8,128)(2,1)} %bh_hbm.1, bf16[512,1024]{1,0:T(8,128)(2,1)} %ph_hbm.1, bf16[1024,1024]{1,0:T(8,128)(2,1)} %proj_hbm.1, s32[16,128]{1,0:T(8,128)} %bitcast.3, ...), custom_call_target="tpu_custom_call" | custom-call | flops 8999999488 | bytes 6000000 | tf_op jit(solution)/shard_map/pallas_call | solution.py:596
  72.6 0.7 copy.14
  73.3 0.6 copy.15
  73.9 1.0 %copy.16 = bf16[512,1024]{1,0:T(8,128)(2,1)} copy(bf16[512,1024]{1,0:T(8,128)(2,1)S(1)} %get-tuple-element.5) | data formatting | bytes 2097152

commit v3 on v2

--- a/solution.py
+++ b/solution.py
@@ -68,7 +68,7 @@
     q_hbm, bh_hbm, ph_hbm, proj_hbm, ids_ref, group_ref, label_ref, lists_ref,
     qg_out, bg_out, pg_out,
     qbuf, proj, bh, ph, pool, column, ot, mask, dense, chosen,
-    ids_byz, ids_in, hs_out, hs_in, d_out, d_in, rows16, idcol, dcol,
+    ids_byz, ids_in, hs_out, hs_in, d_out, d_in, w_out, w_in, rows16, idcol, dcol, wcol, fcol,
     t_buf, o_buf, rs_out, rs_in, dg, part, xr_out, xr_in, xsum, y_out, y_in, gterm,
     contrib, g_send, g_recv, g_own, gb,
     ld_sem, ag_s, ag_r, rs_s, rs_r, xa_s, xa_r, xr_s, xr_r, one_s, one_r, z_ready, xy_ready,
@@ -310,29 +310,22 @@
     xa_arrive(1, 0)
     ag_arrive(5)
     score(6)
+    ag_arrive(6)
+    score(0)
+
+    small_wait(hs_in, one_r.at[1])
+    hard = hs_in[...]
+    hard_top = jnp.max(jnp.max(hard, axis=0), axis=0, keepdims=True)
+    hard = jnp.exp(hard - hard_top[None])
+    hard_sum = jnp.sum(jnp.sum(hard, axis=0), axis=0, keepdims=True)
+    share = (hard / hard_sum[None]).astype(BF16).astype(F32)
+    w_out[...] = share
+    w_in[0] = share[0]
+    for slot in range(1, NZ):
+        small(w_out.at[slot], w_in, 2, slot).start()
     xa_arrive(0, 1)
     xa_arrive(0, 2)
     dense_half(0)
-    ag_arrive(6)
-    score(0)
-    xa_arrive(1, 1)
-    xa_arrive(1, 2)
-    dense_half(1)
-
-    group_max = jnp.max(dense[...], axis=0, keepdims=True)
-    small_wait(hs_in, one_r.at[1])
-    hard = hs_in[...]
-    top = jnp.maximum(group_max, jnp.max(jnp.max(hard, axis=0), axis=0, keepdims=True))
-    hard = jnp.exp(hard - top[None])
-    likely = jnp.where(mask[...] > 0.0, jnp.exp(dense[...] - top), 0.0)
-    total = jnp.sum(likely, axis=0, keepdims=True) + jnp.sum(jnp.sum(hard, axis=0), axis=0, keepdims=True)
-    d_hard = (hard / total[None]).astype(BF16).astype(F32)
-    d_out[...] = d_hard
-    d_in[0] = d_hard[0]
-    for slot in range(1, NZ):
-        small(d_out.at[slot], d_in, 3, slot).start()
-    target = jnp.where(lax.broadcasted_iota(jnp.int32, (NB, QD), 0) == label_row, 1.0, 0.0)
-    dg[...] = (likely / total - target).astype(BF16)
 
     def rs(direction, n):
         return remote(
@@ -360,7 +353,7 @@
             for k in (0, 1):
                 at = 2 * (slot + j) + k
                 hit = lane == idcol[:, at : at + 1]
-                value = jnp.where(hit, dcol[:, at : at + 1], 0.0)
+                value = jnp.where(hit, wcol[:, at : at + 1], 0.0)
                 o_buf[j * QD : (j + 1) * QD, k * PD : (k + 1) * PD] = value.astype(BF16)
 
         def tile(i, carry):
@@ -448,26 +441,50 @@
 
             lax.fori_loop(0, 2, tile, 0)
 
+    small_wait(w_in, one_r.at[2])
+    for slot in range(NZ):
+        rows16[2 * slot : 2 * slot + 2, :] = w_in[slot]
+    wcol[...] = dot_nt(eye(QD), rows16[...].astype(BF16))
+    terms(0)
+    rs_send(0)
+    terms(6)
+    rs_send(1)
+    xa_arrive(1, 1)
+    xa_arrive(1, 2)
+    dense_half(1)
+
+    group_max = jnp.max(dense[...], axis=0, keepdims=True)
+    top = jnp.maximum(group_max, hard_top)
+    hard = jnp.exp(hs_in[...] - top[None])
+    likely = jnp.where(mask[...] > 0.0, jnp.exp(dense[...] - top), 0.0)
+    total = jnp.sum(likely, axis=0, keepdims=True) + jnp.sum(jnp.sum(hard, axis=0), axis=0, keepdims=True)
+    factor = hard_sum * jnp.exp(hard_top - top) / total
+    here = lax.broadcasted_iota(jnp.int32, (QD, QD), 0) == lax.broadcasted_iota(jnp.int32, (QD, QD), 1)
+    fcol[...] = jnp.sum(jnp.where(here, factor, 0.0), axis=1, keepdims=True)
+    d_hard = (hard / total[None]).astype(BF16).astype(F32)
+    d_out[...] = d_hard
+    d_in[0] = d_hard[0]
+    for slot in range(1, NZ):
+        small(d_out.at[slot], d_in, 3, slot).start()
+    target = jnp.where(lax.broadcasted_iota(jnp.int32, (NB, QD), 0) == label_row, 1.0, 0.0)
+    dg[...] = (likely / total - target).astype(BF16)
+
     part_half(0)
     xr_send(0, 0)
     xr_send(0, 1)
     part_half(1)
     xr_send(1, 0)
     xr_send(1, 1)
-    small_wait(d_in, one_r.at[3])
-    for slot in range(NZ):
-        rows16[2 * slot : 2 * slot + 2, :] = d_in[slot]
-    dcol[...] = dot_nt(eye(QD), rows16[...].astype(BF16))
-    terms(0)
-    rs_send(0)
-    terms(6)
-    rs_send(1)
     terms(4)
     rs_send(2)
     terms(2)
     xr_send(0, 2)
     rs_send(3)
     xr_send(1, 2)
+    small_wait(d_in, one_r.at[3])
+    for slot in range(NZ):
+        rows16[2 * slot : 2 * slot + 2, :] = d_in[slot]
+    dcol[...] = dot_nt(eye(QD), rows16[...].astype(BF16))
     contribs(0)
     rs_send(4)
     pool_sum(0, g_send, 0, 4)
@@ -511,8 +528,8 @@
         rs(direction, 6).wait_recv()
     for half in (0, 1):
         rows = slice(half * SUB, (half + 1) * SUB)
-        value = gterm[rows, :] + t_buf[0, rows, :]
-        value = value + (rs_in[half, 6].astype(F32) + rs_in[1 - half, 5].astype(F32))
+        value = t_buf[0, rows, :] + (rs_in[half, 6].astype(F32) + rs_in[1 - half, 5].astype(F32))
+        value = gterm[rows, :] + value * fcol[rows, :]
         qg_out[rows, :] = (value * SCALE).astype(BF16)
 
     for direction in (0, 1):
@@ -525,6 +542,7 @@
                 xr(half, direction, n).wait_send()
     small_wait(ids_in, one_s.at[0])
     small_wait(hs_in, one_s.at[1])
+    small_wait(w_in, one_s.at[2])
     small_wait(d_in, one_s.at[3])
     for half in (0, 1):
         all_wait(column.at[half, pl.ds(0, (NY - 1) * IB)], one_s.at[9 + half])
@@ -554,9 +572,13 @@
         pltpu.VMEM((NZ, 2, QD), F32),
         pltpu.VMEM((NZ, 2, QD), F32),
         pltpu.VMEM((NZ, 2, QD), F32),
+        pltpu.VMEM((NZ, 2, QD), F32),
+        pltpu.VMEM((NZ, 2, QD), F32),
         pltpu.VMEM((HN, QD), F32),
         pltpu.VMEM((QD, HN), jnp.int32),
         pltpu.VMEM((QD, HN), F32),
+        pltpu.VMEM((QD, HN), F32),
+        pltpu.VMEM((QD, 1), F32),
         pltpu.VMEM((NZ, QD, D), F32),
         pltpu.VMEM((2 * QD, 2 * PD), BF16),
         pltpu.VMEM((2, 7, SUB, D), BF16),

time: 75.1 us -> 74.5 us (level)
  no operation moved by 1% of the time
where the time goes in v3:
time: 74.5 us; the launch traced here: 74.3 us
  Pallas kernels  71.3 us (96%)
  local copies, waits for them, and re-layouts  2.29 us (3%)
    pallas_call x1, Pallas kernels, shards(): pl.pallas_call(kernel, out_shape=shapes, in_specs=[hbm] * 4 + [vmem] * 4,...  71.3 us
    unnamed x3, local copies, waits for them, and re-layouts  2.29 us

profile of v3, /device:TPU:6, one launch (start us, length us, event | category | flops | bytes accessed | tf_op | source)
XLA Modules:
  0.0 74.3 jit_solution(9244395940174737928)
XLA Ops:
  0.6 71.3 %shard_map.103 = (bf16[128,1024]{1,0:T(8,128)(2,1)S(1)}, bf16[16,1024]{1,0:T(8,128)(2,1)S(1)}, bf16[512,1024]{1,0:T(8,128)(2,1)S(1)}) custom-call(bf16[128,1024]{1,0:T(8,128)(2,1)} %q_hbm.1, bf16[16,1024]{1,0:T(8,128)(2,1)} %bh_hbm.1, bf16[512,1024]{1,0:T(8,128)(2,1)} %ph_hbm.1, bf16[1024,1024]{1,0:T(8,128)(2,1)} %proj_hbm.1, s32[16,128]{1,0:T(8,128)} %bitcast.3, ...), custom_call_target="tpu_custom_call" | custom-call | flops 8999999488 | bytes 6000000 | tf_op jit(solution)/shard_map/pallas_call | solution.py:618
  72.0 0.7 copy.14
  72.7 0.6 copy.15
  73.3 1.0 %copy.16 = bf16[512,1024]{1,0:T(8,128)(2,1)} copy(bf16[512,1024]{1,0:T(8,128)(2,1)S(1)} %get-tuple-element.5) | data formatting | bytes 2097152

commit v4 on v3

--- a/solution.py
+++ b/solution.py
@@ -172,19 +172,7 @@
             remote(here, here, one_s.at[9 + half], one_r.at[9 + half], at_y(shift)).start()
 
     batch_half(0)
-
-    @pl.when(core == 1)
-    def _():
-        pl.semaphore_wait(barrier, 2 * (NY - 1) + 2 * 2 + 1)
-        pl.semaphore_signal(xy_ready, inc=1, device_id=partner, device_id_type=MESH)
-
-    @pl.when(core == 0)
-    def _():
-        pl.semaphore_wait(xy_ready, 1)
-
-    ya_send(0)
     batch_half(1)
-    ya_send(1)
 
     local_rows = ids_ref[...] - lax.broadcasted_iota(jnp.int32, (HN, QD), 0) * PD
     for owner_z in range(NZ):
@@ -194,6 +182,19 @@
         small(ids_byz.at[(z + slot_shift(slot)) % NZ], ids_in, 0, slot).start()
 
     ag_arrive(0)
+
+    @pl.when(core == 1)
+    def _():
+        pl.semaphore_wait(barrier, 2 * (NY - 1) + 2 * 2 + 1)
+        pl.semaphore_signal(xy_ready, inc=1, device_id=partner, device_id_type=MESH)
+
+    @pl.when(core == 0)
+    def _():
+        pl.semaphore_wait(xy_ready, 1)
+
+    ya_send(0)
+    ya_send(1)
+
     loads[3].wait()
     pool_rows = pl.ds(pl.multiple_of(core * PD, PD), PD)
 
@@ -253,10 +254,9 @@
             if n == 0:
                 xa(part_of, direction, 2).start()
 
-    xa_send(0)
     lax.fori_loop(0, NB // 128, mask_tile, 0)
     ag_arrive(2)
-    xa_send(1)
+    xa_send(0)
     small_wait(ids_in, one_r.at[0])
     for slot in range(NZ):
         rows16[2 * slot : 2 * slot + 2, :] = ids_in[slot].astype(F32)
@@ -303,13 +303,14 @@
 
     score(2)
     ag_arrive(3)
-    xa_arrive(0, 0)
+    xa_send(1)
     score(4)
     ag_arrive(4)
     lax.fori_loop(NB // 128, NB // 64, mask_tile, 0)
-    xa_arrive(1, 0)
+    xa_arrive(0, 0)
     ag_arrive(5)
     score(6)
+    xa_arrive(1, 0)
     ag_arrive(6)
     score(0)
 

time: 74.5 us -> 75.8 us (1.017)
  Pallas kernels: 71.3 us -> 72.6 us
    pallas_call x1, Pallas kernels: 71.3 us -> 72.6 us  [shards(): pl.pallas_call(kernel, out_shape=shapes, in_specs=[hbm] * 4 + [vmem] * 4,...]
where the time goes in v4:
time: 75.8 us; the launch traced here: 75.6 us
  Pallas kernels  72.6 us (96%)
  local copies, waits for them, and re-layouts  2.29 us (3%)
    pallas_call x1, Pallas kernels, shards(): pl.pallas_call(kernel, out_shape=shapes, in_specs=[hbm] * 4 + [vmem] * 4,...  72.6 us
    unnamed x3, local copies, waits for them, and re-layouts  2.29 us

profile of v4, /device:TPU:6, one launch (start us, length us, event | category | flops | bytes accessed | tf_op | source)
XLA Modules:
  0.0 75.6 jit_solution(3777963614390299580)
XLA Ops:
  0.6 72.6 %shard_map.103 = (bf16[128,1024]{1,0:T(8,128)(2,1)S(1)}, bf16[16,1024]{1,0:T(8,128)(2,1)S(1)}, bf16[512,1024]{1,0:T(8,128)(2,1)S(1)}) custom-call(bf16[128,1024]{1,0:T(8,128)(2,1)} %q_hbm.1, bf16[16,1024]{1,0:T(8,128)(2,1)} %bh_hbm.1, bf16[512,1024]{1,0:T(8,128)(2,1)} %ph_hbm.1, bf16[1024,1024]{1,0:T(8,128)(2,1)} %proj_hbm.1, s32[16,128]{1,0:T(8,128)} %bitcast.3, ...), custom_call_target="tpu_custom_call" | custom-call | flops 8999999488 | bytes 6000000 | tf_op jit(solution)/shard_map/pallas_call | solution.py:619
  73.3 0.7 copy.14
  74.0 0.6 copy.15
  74.6 1.0 %copy.16 = bf16[512,1024]{1,0:T(8,128)(2,1)} copy(bf16[512,1024]{1,0:T(8,128)(2,1)S(1)} %get-tuple-element.5) | data formatting | bytes 2097152
